TPU v7x, 256 devices: a whole 4x4x8 slice. The times are simulated.
256 devices in a mesh: dp: 128 (over z, y_lo, x, core), group: 2 (over y_hi).
Axes of the slice: x: 4, y: 4 (y_hi: 2, y_lo: 2; y = y_hi * 2 + y_lo), z: 8, core: 2. Of those that a mesh axis runs over, the one named last changes fastest.
Arguments:
- atom_feats: bfloat16 [2048, 32, 512], P(('dp', 'group')), may hold values from -6 to 6
- coords: float32 [2048, 3, 32], P(('dp', 'group')), may hold values from -6 to 6
- atom_counts: int32 [2048], P(('dp', 'group')), may hold values from 8 to 32
- positives: int32 [2048], P(('dp', 'group')), may hold values from 0 to 2047, each once
- z2: bfloat16 [2048, 128], P(('dp', 'group')), may hold values from -6 to 6
- w_qkv: bfloat16 [512, 1536], replicated, may hold values from -0.25 to 0.25
- w_out: bfloat16 [512, 512], replicated, may hold values from -0.25 to 0.25
- proj: bfloat16 [512, 128], replicated, may hold values from -0.25 to 0.25
- bias_weight: float32 [128, 64], replicated, may hold values from -2 to 36
- ln_gain: float32 [512], replicated, may hold values from 0.5 to 1.5
Outputs:
- loss: float32 [], replicated
- grad_z2: float32 [2048, 128], P(('dp', 'group'))
- grad_w_qkv: float32 [512, 1536], replicated
- grad_w_out: float32 [512, 512], replicated
- grad_proj: float32 [512, 128], replicated
- grad_bias_weight: float32 [128, 64], replicated
- grad_ln_gain: float32 [512], replicated
Inputs may be any that keep to these rules, and one draw needn't show every extreme that they name: positives is a permutation of the 2048 molecules.
All inputs are finite; a program needn't handle non-finite values.
Results may differ from a plain program's by a relative error of at most 0.014.
Values may be sent and summed in bfloat16 or wider, within the bound.
A program may use at most 128 MiB of HBM per device.

v0:
```python
import math
import jax
import jax.numpy as jnp
from jax import lax
from jax.sharding import PartitionSpec as P


def pair_distance(coords):
    offsets = coords[:, :, :, None] - coords[:, :, None, :]
    return jnp.sqrt(jnp.sum(offsets * offsets, axis=1) + 0.25)


def kernel_values(distance, kernels):
    centers = jnp.arange(kernels).astype(jnp.float32) * (12.0 / kernels)
    return jnp.exp(-(((distance[..., None] - centers) / 0.5) ** 2))


def group_split(values, width):
    return values.reshape((values.shape[0] // width, width) + values.shape[1:])


def bias_forward(distance, bias_weight):
    mol_count = distance.shape[0]
    width = math.gcd(mol_count, 8)

    def one_group(group_distance):
        basis = kernel_values(group_distance, bias_weight.shape[0])
        return jnp.einsum("mijk,kh->mhij", basis, bias_weight, precision=lax.Precision.HIGHEST)

    biased = lax.map(one_group, group_split(distance, width))
    return biased.reshape((mol_count,) + biased.shape[2:])


def bias_backward(distance, bias_slope, kernels):
    width = math.gcd(distance.shape[0], 8)

    def add_group(running, pieces):
        basis = kernel_values(pieces[0], kernels)
        return (
            running
            + jnp.einsum("mijk,mhij->kh", basis, pieces[1], precision=lax.Precision.HIGHEST),
            None,
        )

    start_sum = jnp.zeros((kernels, bias_slope.shape[1]), jnp.float32)
    summed, unused = lax.scan(
        add_group, start_sum, (group_split(distance, width), group_split(bias_slope, width))
    )
    return summed


def encode_core(params_in, pair_bias, feats, counts):
    w_qkv, w_out, proj, ln_gain = params_in
    mol_count, atom_count, model_width = feats.shape
    head_count = pair_bias.shape[1]
    head_dim = model_width // head_count
    inputs = feats.astype(jnp.float32)
    center = jnp.mean(inputs, axis=-1, keepdims=True)
    spread = jnp.mean((inputs - center) ** 2, axis=-1, keepdims=True)
    normed = ((inputs - center) * lax.rsqrt(spread + 1e-05) * ln_gain).astype(jnp.bfloat16)
    projected = jnp.dot(
        normed.reshape(mol_count * atom_count, model_width),
        w_qkv,
        preferred_element_type=jnp.float32,
    ).astype(jnp.bfloat16)
    projected = projected.reshape(mol_count, atom_count, 3, head_count, head_dim)
    query_heads = projected[:, :, 0]
    key_heads = projected[:, :, 1]
    value_heads = projected[:, :, 2]
    scores = (
        jnp.einsum("mihd,mjhd->mhij", query_heads, key_heads, preferred_element_type=jnp.float32)
        * head_dim ** (-0.5)
        + pair_bias
    )
    is_valid = jnp.arange(atom_count)[None, :] < counts[:, None]
    scores = jnp.where(is_valid[:, None, None, :], scores, -1e30)
    highest = jnp.max(scores, axis=-1, keepdims=True)
    expo = jnp.exp(scores - highest)
    attn_weights = (expo / jnp.sum(expo, axis=-1, keepdims=True)).astype(jnp.bfloat16)
    context = jnp.einsum(
        "mhij,mjhd->mihd", attn_weights, value_heads, preferred_element_type=jnp.float32
    ).astype(jnp.bfloat16)
    hidden = inputs + jnp.dot(
        context.reshape(mol_count * atom_count, model_width),
        w_out,
        preferred_element_type=jnp.float32,
    ).reshape(mol_count, atom_count, model_width)
    pooled = jnp.sum(jnp.where(is_valid[..., None], hidden, 0.0), axis=1)
    return jnp.dot(pooled.astype(jnp.bfloat16), proj, preferred_element_type=jnp.float32)


def unit_rows(values):
    inverse = lax.rsqrt(jnp.mean(values * values, axis=1, keepdims=True) + 1e-06) * values.shape[
        1
    ] ** (-0.5)
    return (values * inverse, inverse)


def unit_backward(values, inverse, grad):
    along = jnp.sum(values * grad, axis=1, keepdims=True)
    return inverse * (grad - values * along * (inverse * inverse))


def on_device(
    atom_feats, coords, atom_counts, positives, z2, w_qkv, w_out, proj, bias_weight, ln_gain
):
    distance = pair_distance(coords)
    pair_bias = bias_forward(distance, bias_weight)

    def local_encode(params_in, bias_in):
        return encode_core(params_in, bias_in, atom_feats, atom_counts)

    z3, pullback = jax.vjp(local_encode, (w_qkv, w_out, proj, ln_gain), pair_bias)
    unit, inverse = unit_rows(z3)
    z3_half = unit.astype(jnp.bfloat16)
    z2_all = lax.all_gather(z2, ("dp", "group"), axis=0, tiled=True)
    batch_rows = z2_all.shape[0]
    logits = jnp.dot(z3_half, z2_all.T, preferred_element_type=jnp.float32)
    expo = jnp.exp(logits)
    row_lse = jnp.log(jnp.sum(expo, axis=1))
    columns = jnp.arange(batch_rows)
    is_positive = positives[:, None] == columns[None, :]
    positive_score = jnp.sum(jnp.where(is_positive, logits, 0.0), axis=1)
    local_sum = jnp.sum(0.5 * row_lse - positive_score)
    col_total = lax.psum(jnp.sum(expo, axis=0), ("dp", "group"))
    col_lse = jnp.log(col_total)
    column_part = 0.5 * jnp.sum(col_lse)
    slope = (
        0.5 * jnp.exp(logits - row_lse[:, None])
        + 0.5 * jnp.exp(logits - col_lse[None, :])
        - is_positive.astype(jnp.float32)
    ).astype(jnp.bfloat16)
    grad_z2 = lax.psum_scatter(
        lax.dot_general(
            slope, z3_half, (((0,), (0,)), ((), ())), preferred_element_type=jnp.float32
        ),
        ("dp", "group"),
        scatter_dimension=0,
        tiled=True,
    )
    grad_unit = jnp.dot(slope, z2_all, preferred_element_type=jnp.float32)
    grad_z3 = unit_backward(z3, inverse, grad_unit)
    pieces, bias_slope = pullback(grad_z3)
    grad_bias = bias_backward(distance, bias_slope, bias_weight.shape[0])
    totals = lax.psum(
        (
            local_sum,
            pieces[0].astype(jnp.float32),
            pieces[1].astype(jnp.float32),
            pieces[2].astype(jnp.float32),
            grad_bias,
            pieces[3],
        ),
        ("dp", "group"),
    )
    loss = (totals[0] + column_part) / batch_rows
    return (loss, grad_z2, totals[1], totals[2], totals[3], totals[4], totals[5])


def solution(mesh):
    return jax.shard_map(
        on_device,
        mesh=mesh,
        in_specs=(
            P(("dp", "group"), None, None),
            P(("dp", "group"), None, None),
            P(("dp", "group")),
            P(("dp", "group")),
            P(("dp", "group"), None),
            P(),
            P(),
            P(),
            P(),
            P(),
        ),
        out_specs=(P(), P(("dp", "group"), None), P(), P(), P(), P(), P()),
        check_vma=False,
    )
```

profile of v0, /device:TPU:97, one launch (start us, length us, event | category | flops | bytes accessed | tf_op | source)
XLA Modules:
  0.0 1103.0 jit_solution(12725409746250518894)
XLA Ops:
  7.2 1.2 convert_reduce_fusion.1
  8.4 1.2 fusion.44
  9.6 1.1 fusion.42
  10.7 0.7 copy-done.13
  12.3 2.8 reshape.179
  15.1 3.9 fusion.58
  19.5 0.6 copy-done.21
  20.1 5.4 fusion.10
  25.5 9.2 copy.77
  34.7 7.3 fusion.60
  41.9 2.7 fusion.9
  45.2 2.3 divide_convert_fusion
  47.5 1.2 convolution_convert_fusion.4
  49.9 569.9 %all_gather.3 = bf16[2048,128]{1,0:T(8,128)(2,1)S(1)} all-gather(bf16[8,128]{1,0:T(8,128)(2,1)S(1)} %copy-done.25), channel_id=1, replica_groups=mesh['dp'=128,'group'=2] {'dp','group'}, dimensions={0}, use_global_device_ids=true | all-gather | bytes 526336 | tf_op jit(solution)/shard_map/all_gather | solution.py:116
  619.8 0.8 copy-done.12
  621.1 130.1 %psum.50 = f32[2048]{0:T(1024)S(1)} all-reduce(f32[2048]{0:T(1024)S(1)} %get-tuple-element.27), channel_id=1, replica_groups=mesh['dp'=128,'group'=2] {'dp','group'}, use_global_device_ids=true, to_apply=%region_12.13 | all-reduce | flops 2048 | bytes 16384 | tf_op jit(solution)/shard_map/psum | solution.py:125
  751.7 0.6 fusion.59
  752.3 1.4 multiply_reduce_fusion.1
  753.7 1.0 fusion.32
  754.7 1.1 fusion.34
  755.9 0.8 multiply_divide_fusion
  756.6 0.8 broadcast_select_fusion
  757.5 2.1 fusion.61
  759.6 1.8 copy.80
  761.4 2.4 reshape.180
  763.8 5.9 fusion.21
  769.8 5.8 fusion.3
  775.7 8.8 convert_reduce_fusion
  784.5 6.1 add_select_fusion
  790.6 3.7 fusion.25
  794.4 2.2 fusion.22
  796.5 1.4 fusion.53
  798.0 1.2 copy.87
  799.2 0.7 reshape.182
  799.9 2.7 pad_add_fusion
  802.6 5.3 copy.86
  807.9 4.3 reshape.181
  812.2 2.3 fusion.14
  814.5 1.3 fusion.28
  815.8 0.6 fusion.43
  816.4 8.8 copy.88
  825.2 10.3 fusion.33
  835.5 74.4 %all-reduce.4 = (f32[]{:T(128)}, f32[128,64]{0,1:T(8,128)}, f32[512]{0:T(512)}) all-reduce(f32[]{:T(128)} %get-tuple-element.52, f32[128,64]{0,1:T(8,128)S(1)} %fusion.33, f32[512]{0:T(512)S(1)} %fusion.43), channel_id=1, replica_groups=mesh['dp'=128,'group'=2] {'dp','group'}, use_global_device_ids=true, to_apply=%region_10.11 | all-reduce | flops 8705 | bytes 69640 | tf_op jit(solution)/shard_map/psum | solution.py:145
  911.2 176.8 %all-reduce.8.cloned.1.call-done = (f32[2048,128]{1,0:T(8,128)}, f32[512,1536]{1,0:T(8,128)}, f32[512,512]{1,0:T(8,128)}, f32[512,128]{1,0:T(8,128)}) async-done(((f32[2048,128]{1,0:T(8,128)}, f32[512,1536]{1,0:T(8,128)}, f32[512,512]{1,0:T(8,128)}, f32[512,128]{1,0:T(8,128)}), (f32[2048,128]{1,0:T(8,128)}, f32[512,1536]{1,0:T(8,128)}, f32[512,512]{1,0:T(8,128)}, ...) | async-done | bytes 5505040
  1088.0 1.4 constant_dynamic-slice_fusion
  1089.3 3.8 copy.126
  1093.1 1.0 copy.127
  1094.1 0.7 copy.128
  (79 shorter events, 4.4 us)
Async XLA Ops:
  7.2 4.3 copy-start
  7.2 1080.8 %all-reduce.8.cloned.1.call-start = ((), (), s32[]{:S(2)}) async-start(), calls=%async_computation | async-start | bytes 11010048
  10.7 0.7 copy-start.13
  12.3 6.8 copy-start.27
  12.3 6.9 copy-start.23
  15.1 5.0 copy-start.26
  19.5 0.6 copy-start.21
  41.9 3.2 copy-start.1
  45.2 2.3 copy-start.9
  47.4 572.4 %copy-start.3 = (bf16[8,64,32,32]{2,3,1,0:T(8,128)(2,1)}, bf16[8,64,32,32]{2,3,1,0:T(8,128)(2,1)S(1)}, u32[]{:S(2)}) copy-start(bf16[8,64,32,32]{2,3,1,0:T(8,128)(2,1)S(1)} %divide_convert_fusion) | copy-start | bytes 3145732
  47.4 1.3 copy-start.11
  47.5 1.7 copy-start.15
  47.5 2.1 copy-start.20
  47.5 2.4 copy-start.25
  47.5 573.1 %copy-start.24 = (s32[8]{0:T(128)S(1)}, s32[8]{0:T(128)}, u32[]{:S(2)}) copy-start(s32[8]{0:T(128)} %param.13) | copy-start | bytes 100
  49.1 570.7 %copy-start.6 = (bf16[8,64,8,32]{3,2,1,0:T(8,128)(2,1)}, bf16[8,64,8,32]{3,2,1,0:T(8,128)(2,1)S(1)}, u32[]{:S(2)}) copy-start(bf16[8,64,8,32]{3,2,1,0:T(8,128)(2,1)S(1)} %convolution_convert_fusion.4) | copy-start | bytes 786436
  619.8 0.8 copy-start.12
  763.8 5.9 copy-start.8
  763.8 5.9 copy-start.10
  763.8 5.9 copy-start.16
  763.8 11.8 %slice-start = ((s8[8388608]{0:T(1024)(128)(4,1)}), s8[4194304]{0:T(1024)(128)(4,1)S(1)}, s32[]{:S(2)}) async-start(s8[8388608]{0:T(1024)(128)(4,1)} %bitcast.90), calls=%async_computation.1 | async-start | bytes 8388608
  769.8 5.9 slice-start.1
  775.6 8.8 copy-start.4
  784.5 6.1 copy-start.5
  790.6 3.7 copy-start.2
  794.4 3.6 copy-start.7
  802.6 9.6 copy-start.14
  807.9 6.6 copy-start.18
  816.4 8.8 copy-start.22
  1088.0 5.2 copy-start.17
  1089.3 4.8 copy-start.19
Sparse Core Ops, SparseCore 0:
  815.9 272.0 all-reduce.7
where the time goes:
time: 1110 us; the launch traced here: 1100 us
  blocking collectives  774 us (70%)
  waiting for transfers between devices  177 us (16%)
  matrix products  54.6 us (5%)
  local copies, waits for them, and re-layouts  50.9 us (5%)
  other arithmetic  29.1 us (3%)
  between operations  17.1 us (2%)
    all_gather x1, blocking collectives, on_device(): z2_all = lax.all_gather(z2, ('dp', 'group'), axis=0, tiled=True)  570 us
    unnamed x2, waiting for transfers between devices  177 us
    psum x1, blocking collectives, on_device(): col_total = lax.psum(jnp.sum(expo, axis=0), ('dp', 'group'))  130 us
    psum x1, blocking collectives, on_device(): lax.psum((local_sum, pieces[0].astype(jnp.float32), pieces[1].astype(jnp....  74.4 us
  transfers between devices with their start and end apart: 1, of which 1 were waited for; matrix products, arithmetic and copies ran while one was open for 2% of the time, Pallas kernels for 0%

commit v1 on v0

--- a/solution.py
+++ b/solution.py
@@ -143,15 +143,18 @@
     pieces, bias_slope = pullback(grad_z3)
     grad_bias = bias_backward(distance, bias_slope, bias_weight.shape[0])
     totals = lax.psum(
-        (
-            local_sum,
-            pieces[0].astype(jnp.float32),
-            pieces[1].astype(jnp.float32),
-            pieces[2].astype(jnp.float32),
-            grad_bias,
-            pieces[3],
+        lax.psum(
+            (
+                local_sum,
+                pieces[0].astype(jnp.float32),
+                pieces[1].astype(jnp.float32),
+                pieces[2].astype(jnp.float32),
+                grad_bias,
+                pieces[3],
+            ),
+            "group",
         ),
-        ("dp", "group"),
+        "dp",
     )
     loss = (totals[0] + column_part) / batch_rows
     return (loss, grad_z2, totals[1], totals[2], totals[3], totals[4], totals[5])

time: 1110 us -> 2310 us (2.08); the launches traced: 1100 us -> 2270 us
  waiting for transfers between devices: 177 us -> 892 us
  blocking collectives: 774 us -> 1220 us
    psum x0 -> x2, waiting for transfers between devices: none -> 892 us  [the longest x1 769 us: on_device(): lax.psum(lax.psum((local_sum, pieces[0].astype(jnp.float32), pieces[1].as...]
    psum x0 -> x1, blocking collectives: none -> 513 us  [on_device(): lax.psum(lax.psum((local_sum, pieces[0].astype(jnp.float32), pieces[1].as...]
    unnamed x2 -> x4, waiting for transfers between devices: 177 us -> 0.07 us
    psum x1, blocking collectives: 74.4 us -> 8.11 us  [on_device(): lax.psum((local_sum, pieces[0].astype(jnp.float32), pieces[1].astype(jnp....]
  transfers between devices with their start and end apart: 1 -> 3, of which waited for: 1 -> 2; matrix products, arithmetic and copies ran while one was open for 2% -> 1% of each run, Pallas kernels for 0% -> 0%
where the time goes in v1:
time: 2310 us; the launch traced here: 2270 us
  blocking collectives  1220 us (53%)
  waiting for transfers between devices  892 us (39%)
  matrix products  54.7 us (2%)
  local copies, waits for them, and re-layouts  50.5 us (2%)
  other arithmetic  29.5 us (1%)
    psum x1, waiting for transfers between devices, on_device(): lax.psum(lax.psum((local_sum, pieces[0].astype(jnp.float32), pieces[1].as...  769 us
    all_gather x1, blocking collectives, on_device(): z2_all = lax.all_gather(z2, ('dp', 'group'), axis=0, tiled=True)  570 us
    psum x1, blocking collectives, on_device(): lax.psum(lax.psum((local_sum, pieces[0].astype(jnp.float32), pieces[1].as...  513 us
    psum x1, blocking collectives, on_device(): col_total = lax.psum(jnp.sum(expo, axis=0), ('dp', 'group'))  130 us
    psum x1, waiting for transfers between devices, on_device(): lax.psum((local_sum, pieces[0].astype(jnp.float32), pieces[1].astype(jnp....  123 us
  transfers between devices with their start and end apart: 3, of which 2 were waited for; matrix products, arithmetic and copies ran while one was open for 1% of the time, Pallas kernels for 0%

profile of v1, /device:TPU:97, one launch (start us, length us, event | category | flops | bytes accessed | tf_op | source)
XLA Modules:
  0.0 2265.9 jit_solution(8451897206577520215)
XLA Ops:
  7.2 0.8 iota_compare_fusion.1
  8.2 1.1 convert_reduce_fusion.1
  9.2 1.2 fusion.44
  10.4 0.7 copy.73
  11.5 1.2 fusion.42
  14.2 2.8 reshape.179
  17.0 4.2 fusion.58
  21.2 5.4 fusion.10
  26.6 9.2 copy.77
  35.7 7.3 fusion.60
  43.0 2.7 fusion.9
  45.7 0.8 multiply_divide_fusion
  46.5 2.1 divide_convert_fusion
  48.6 570.4 %all_gather.3 = bf16[2048,128]{1,0:T(8,128)(2,1)S(1)} all-gather(bf16[8,128]{1,0:T(8,128)(2,1)S(1)} %copy-done.24), channel_id=1, replica_groups=mesh['dp'=128,'group'=2] {'dp','group'}, dimensions={0}, use_global_device_ids=true | all-gather | bytes 526336 | tf_op jit(solution)/shard_map/all_gather | solution.py:116
  619.1 1.2 convolution_convert_fusion.4
  621.7 130.1 %psum.93 = f32[2048]{0:T(1024)S(1)} all-reduce(f32[2048]{0:T(1024)S(1)} %get-tuple-element.27), channel_id=1, replica_groups=mesh['dp'=128,'group'=2] {'dp','group'}, use_global_device_ids=true, to_apply=%region_13.14 | all-reduce | flops 2048 | bytes 16384 | tf_op jit(solution)/shard_map/psum | solution.py:125
  753.0 1.4 multiply_reduce_fusion.1
  754.4 1.1 fusion.34
  755.5 1.0 fusion.32
  756.5 0.8 broadcast_select_fusion
  757.4 2.1 fusion.61
  759.5 1.8 copy.80
  761.3 2.4 reshape.180
  763.7 5.9 fusion.21
  769.6 5.8 fusion.3
  775.5 8.8 convert_reduce_fusion
  784.4 5.9 add_select_fusion
  790.3 2.7 fusion.22
  793.0 0.8 copy-done.2
  793.8 3.3 fusion.25
  797.1 1.2 copy.87
  798.3 0.7 reshape.182
  799.0 2.7 pad_add_fusion
  801.7 5.3 copy.86
  807.0 4.1 reshape.181
  811.1 2.3 fusion.14
  813.4 1.3 fusion.28
  814.8 1.4 fusion.53
  816.2 123.2 %all-reduce.16.cloned.1.call-done = (f32[512,1536]{1,0:T(8,128)}, f32[512,512]{1,0:T(8,128)}, f32[512,128]{1,0:T(8,128)}) async-done(((f32[512,1536]{1,0:T(8,128)}, f32[512,512]{1,0:T(8,128)}, f32[512,128]{1,0:T(8,128)}), (f32[512,1536]{1,0:T(8,128)}, f32[512,512]{1,0:T(8,128)}, f32[512,128]{1,0:T(8,128)})) %all-reduce.16.cloned.1.call-update) | async-done | bytes 4456464 | tf_op jit(solution)/shard_map/psum | solution.py:146
  939.5 9.0 copy.88
  949.1 10.3 fusion.33
  959.4 8.1 all-reduce.6
  967.5 513.1 %all-reduce.4 = (f32[]{:T(128)}, f32[128,64]{0,1:T(8,128)}, f32[512]{0:T(512)}) all-reduce(f32[]{:T(128)} %get-tuple-element.40, f32[128,64]{0,1:T(8,128)S(1)} %get-tuple-element.41, f32[512]{0:T(512)S(1)} %get-tuple-element.42), channel_id=1, replica_groups=mesh['dp'=128,'group'=2] {'dp'}, use_global_device_ids=true, to_apply=%region_11.12 | all-reduce | flops 8705 | bytes 69640 | tf_op jit(solution)/shard_map/psum | solution.py:145
  1481.9 1.3 constant_dynamic-slice_fusion
  1483.2 769.1 %all-reduce.14.cloned.1.call-done = (f32[512,1536]{1,0:T(8,128)}, f32[512,512]{1,0:T(8,128)}, f32[512,128]{1,0:T(8,128)}) async-done(((f32[512,1536]{1,0:T(8,128)}, f32[512,512]{1,0:T(8,128)}, f32[512,128]{1,0:T(8,128)}), (f32[512,1536]{1,0:T(8,128)}, f32[512,512]{1,0:T(8,128)}, f32[512,128]{1,0:T(8,128)})) %all-reduce.14.cloned.1.call-update) | async-done | bytes 4456464 | tf_op jit(solution)/shard_map/psum | solution.py:145
  2252.3 3.9 copy.129
  2256.2 1.0 copy.130
  2257.1 0.7 copy.131
  (82 shorter events, 5.6 us)
Async XLA Ops:
  7.2 6.2 copy-start
  7.2 932.3 %all-reduce.16.cloned.1.call-start = ((), (), s32[]{:S(2)}) async-start(), calls=%async_computation.2 | async-start | bytes 8912896 | tf_op jit(solution)/shard_map/psum | solution.py:146
  11.4 9.7 copy-start.21
  12.6 0.7 copy-start.13
  14.2 7.0 copy-start.25
  43.0 3.5 copy-start.1
  46.5 2.1 copy-start.24
  46.5 572.6 %copy-start.9 = (bf16[8,32,1,64,8]{1,0,4,3,2:T(8,128)(2,1)S(1)}, bf16[8,32,1,64,8]{1,0,4,3,2:T(8,128)(2,1)}, u32[]{:S(2)}) copy-start(bf16[8,32,1,64,8]{1,0,4,3,2:T(8,128)(2,1)} %get-tuple-element.49) | copy-start | bytes 786436
  48.6 572.2 %copy-start.3 = (bf16[8,64,32,32]{2,3,1,0:T(8,128)(2,1)}, bf16[8,64,32,32]{2,3,1,0:T(8,128)(2,1)S(1)}, u32[]{:S(2)}) copy-start(bf16[8,64,32,32]{2,3,1,0:T(8,128)(2,1)S(1)} %divide_convert_fusion) | copy-start | bytes 3145732
  48.6 571.7 %copy-start.11 = (bf16[8,32,512]{2,1,0:T(8,128)(2,1)S(1)}, bf16[8,32,512]{2,1,0:T(8,128)(2,1)}, u32[]{:S(2)}) copy-start(bf16[8,32,512]{2,1,0:T(8,128)(2,1)} %param.10) | copy-start | bytes 786436
  48.6 571.7 %copy-start.15 = (bf16[512,512]{1,0:T(8,128)(2,1)S(1)}, bf16[512,512]{1,0:T(8,128)(2,1)}, u32[]{:S(2)}) copy-start(bf16[512,512]{1,0:T(8,128)(2,1)} %param.16) | copy-start | bytes 1572868
  619.1 2.7 copy-start.12
  619.1 1.7 copy-start.20
  619.1 2.2 copy-start.23
  620.3 1.0 copy-start.6
  763.7 5.9 copy-start.8
  763.7 5.9 copy-start.10
  763.7 5.9 copy-start.16
  763.7 11.8 slice-start
  769.6 5.9 slice-start.1
  775.5 8.8 copy-start.4
  784.4 5.9 copy-start.5
  790.2 3.6 copy-start.2
  793.8 3.3 copy-start.7
  801.7 9.4 copy-start.14
  807.0 6.4 copy-start.18
  814.7 667.2 %all-reduce.12.cloned.1.call-start = ((), (), s32[]{:S(2)}) async-start(), calls=%async_computation | async-start | bytes 2097152
  816.2 1436.1 %all-reduce.14.cloned.1.call-start = ((), (), s32[]{:S(2)}) async-start(), calls=%async_computation.1 | async-start | bytes 8912896 | tf_op jit(solution)/shard_map/psum | solution.py:145
  939.5 9.6 copy-start.22
  2252.3 3.9 copy-start.17
  2252.3 4.8 copy-start.19
Sparse Core Ops, SparseCore 0:
  814.8 124.5 all-reduce.15
  946.3 256.4 all-reduce.11
  1205.7 1046.5 all-reduce.13
